TPU v7x, 256 devices: a whole 4x4x8 slice. The times are simulated.
256 devices in a mesh: rows: 64 (over y, x, z_lo, core), cols: 4 (over z_hi).
Axes of the slice: x: 4, y: 4, z: 8 (z_hi: 4, z_lo: 2; z = z_hi * 2 + z_lo), core: 2. Of those that a mesh axis runs over, the one named last changes fastest.
Arguments:
- noise: bfloat16 [32768, 4096], P('rows'), may hold values from -12 to 12
- data: bfloat16 [4096, 4096], P('cols', 'rows'), may hold values from -12 to 12
Outputs:
- targets: bfloat16 [32768, 4096], P('rows', 'cols')
- row_potential: float32 [32768], P('rows')
- col_potential: float32 [4096], P('cols')
All inputs are finite; a program needn't handle non-finite values.
Results may differ from a plain program's by a relative error of at most 0.012.
Values may be sent and summed in bfloat16 or wider, within the bound.
A program may use at most 64 MiB of HBM per device.

v0:
```python
import math

import jax
import jax.numpy as jnp
from jax import lax
from jax.sharding import PartitionSpec as P

ITERS = 4


EPSILON = 0.05


def row_lse(scores):
    local_max = jnp.max(scores, axis=1)
    local_sum = jnp.sum(jnp.exp(scores - local_max[:, None]), axis=1)
    top = lax.pmax(local_max, "cols")
    total = lax.psum(local_sum * jnp.exp(local_max - top), "cols")
    return top + jnp.log(total)


def col_lse(scores):
    local_max = jnp.max(scores, axis=0)
    local_sum = jnp.sum(jnp.exp(scores - local_max[None, :]), axis=0)
    top = lax.pmax(local_max, "rows")
    total = lax.psum(local_sum * jnp.exp(local_max - top), "rows")
    return top + jnp.log(total)


def contract_rows(left, right):
    return lax.dot_general(
        left, right, (((1,), (1,)), ((), ())), preferred_element_type=jnp.float32
    )


def per_device(noise, data):
    row_count = noise.shape[0]
    col_count = data.shape[0]
    latent_width = noise.shape[1]
    log_rows = -math.log(row_count * lax.axis_size("rows"))
    log_cols = -math.log(col_count * lax.axis_size("cols"))
    noise_sq = jnp.sum(jnp.square(noise.astype(jnp.float32)), axis=1)
    whole = lax.all_gather(data, "rows", axis=1, tiled=True)
    gram = contract_rows(noise, whole)
    data_sq = jnp.sum(jnp.square(whole.astype(jnp.float32)), axis=1)
    cost = (noise_sq[:, None] + data_sq[None, :] - 2.0 * gram) / latent_width
    col_potential = jnp.zeros((col_count,), jnp.float32)
    row_potential = jnp.zeros((row_count,), jnp.float32)
    for step in range(ITERS):
        row_potential = EPSILON * (log_rows - row_lse((col_potential[None, :] - cost) / EPSILON))
        col_potential = EPSILON * (log_cols - col_lse((row_potential[:, None] - cost) / EPSILON))
    logits = (col_potential[None, :] - cost) / EPSILON
    weights = jnp.exp(logits - row_lse(logits)[:, None]).astype(jnp.bfloat16)
    partial_targets = jnp.dot(weights, whole, preferred_element_type=jnp.float32)
    targets = lax.psum_scatter(
        partial_targets.astype(jnp.bfloat16), "cols", scatter_dimension=1, tiled=True
    )
    return (targets, row_potential, col_potential)


def solution(mesh):
    in_specs = (P("rows", None), P("cols", "rows"))
    out_specs = (P("rows", "cols"), P("rows"), P("cols"))
    return jax.shard_map(
        per_device, mesh=mesh, in_specs=in_specs, out_specs=out_specs, check_vma=False
    )
```

profile of v0, /device:TPU:1, one launch (start us, length us, event | category | flops | bytes accessed | tf_op | source)
XLA Modules:
  0.0 1455.5 jit_solution(11823357725432081880)
XLA Ops:
  7.2 0.0 all-gather.2.cloned.1.call-start
  7.2 0.7 all-gather.2.cloned.1.call-update
  7.9 0.0 reduce-scatter.2.cloned.1.call-start
  7.9 3.1 multiply_reduce_fusion.1
  11.0 116.7 %all-gather.2.cloned.1.call-done = bf16[1024,4096]{0,1:T(8,128)(2,1)} async-done(((bf16[1024,64]{0,1:T(8,128)(2,1)}), bf16[1024,4096]{0,1:T(8,128)(2,1)}) %all-gather.2.cloned.1.call-update) | async-done | bytes 8388624 | tf_op jit(solution)/shard_map/all_gather | solution.py:43
  127.7 0.0 copy-start
  127.7 5.2 multiply_reduce_fusion
  132.9 0.5 copy-done
  133.5 6.8 fusion
  140.3 10.4 pmax.63
  150.7 0.6 exponential_reduce_fusion.8
  151.2 8.9 psum.63
  160.2 0.3 fusion.1
  160.5 0.5 exponential_reduce_fusion.7
  161.0 142.0 %pmax.64 = f32[1024]{0:T(1024)S(1)} all-reduce(f32[1024]{0:T(1024)S(1)} %fusion.1), channel_id=1, replica_groups=mesh['rows'=64,'cols'=4] {'rows'}, use_global_device_ids=true, to_apply=%region_7.0 | all-reduce | flops 1024 | bytes 8192 | tf_op jit(solution)/shard_map/pmax | solution.py:25
  302.9 138.4 %psum.64 = f32[1024]{0:T(1024)S(1)} all-reduce(f32[1024]{0:T(1024)S(1)} %exponential_multiply_fusion.3), channel_id=1, replica_groups=mesh['rows'=64,'cols'=4] {'rows'}, use_global_device_ids=true, to_apply=%region_9.0 | all-reduce | flops 1024 | bytes 8192 | tf_op jit(solution)/shard_map/psum | solution.py:26
  441.4 0.3 fusion.2
  441.7 0.6 exponential_reduce_fusion.6
  442.3 7.4 pmax.65
  449.7 8.8 psum.65
  458.4 0.3 fusion.3
  458.7 0.5 exponential_reduce_fusion.5
  459.2 142.5 %pmax.66 = f32[1024]{0:T(1024)S(1)} all-reduce(f32[1024]{0:T(1024)S(1)} %fusion.3), channel_id=1, replica_groups=mesh['rows'=64,'cols'=4] {'rows'}, use_global_device_ids=true, to_apply=%region_15.0 | all-reduce | flops 1024 | bytes 8192 | tf_op jit(solution)/shard_map/pmax | solution.py:25
  601.7 138.4 %psum.66 = f32[1024]{0:T(1024)S(1)} all-reduce(f32[1024]{0:T(1024)S(1)} %exponential_multiply_fusion.2), channel_id=1, replica_groups=mesh['rows'=64,'cols'=4] {'rows'}, use_global_device_ids=true, to_apply=%region_17.0 | all-reduce | flops 1024 | bytes 8192 | tf_op jit(solution)/shard_map/psum | solution.py:26
  740.1 0.3 fusion.4
  740.4 0.6 exponential_reduce_fusion.4
  741.0 8.6 pmax.67
  749.6 8.8 psum.67
  758.4 0.3 fusion.5
  758.7 0.5 exponential_reduce_fusion.3
  759.2 142.5 %pmax.68 = f32[1024]{0:T(1024)S(1)} all-reduce(f32[1024]{0:T(1024)S(1)} %fusion.5), channel_id=1, replica_groups=mesh['rows'=64,'cols'=4] {'rows'}, use_global_device_ids=true, to_apply=%region_23.0 | all-reduce | flops 1024 | bytes 8192 | tf_op jit(solution)/shard_map/pmax | solution.py:25
  901.7 138.4 %psum.68 = f32[1024]{0:T(1024)S(1)} all-reduce(f32[1024]{0:T(1024)S(1)} %exponential_multiply_fusion.1), channel_id=1, replica_groups=mesh['rows'=64,'cols'=4] {'rows'}, use_global_device_ids=true, to_apply=%region_25.0 | all-reduce | flops 1024 | bytes 8192 | tf_op jit(solution)/shard_map/psum | solution.py:26
  1040.1 0.3 fusion.6
  1040.4 0.6 exponential_reduce_fusion.2
  1041.0 7.4 pmax.69
  1048.3 9.0 psum.69
  1057.3 0.0 copy-start.2
  1057.3 0.3 fusion.7
  1057.6 142.5 %pmax.70 = f32[1024]{0:T(1024)S(1)} all-reduce(f32[1024]{0:T(1024)S(1)} %fusion.7), channel_id=1, replica_groups=mesh['rows'=64,'cols'=4] {'rows'}, use_global_device_ids=true, to_apply=%region_31.0 | all-reduce | flops 1024 | bytes 8192 | tf_op jit(solution)/shard_map/pmax | solution.py:25
  1200.1 0.5 exponential_reduce_fusion.1
  1200.6 0.0 copy-done.2
  1200.6 138.4 %psum.70 = f32[1024]{0:T(1024)S(1)} all-reduce(f32[1024]{0:T(1024)S(1)} %exponential_multiply_fusion), channel_id=1, replica_groups=mesh['rows'=64,'cols'=4] {'rows'}, use_global_device_ids=true, to_apply=%region_33.0 | all-reduce | flops 1024 | bytes 8192 | tf_op jit(solution)/shard_map/psum | solution.py:26
  1339.1 0.0 copy-start.1
  1339.1 0.3 fusion.8
  1339.3 8.5 pmax.71
  1347.9 0.6 exponential_reduce_fusion
  1348.4 8.8 psum.71
  1357.3 0.0 copy-done.1
  1357.3 9.6 convolution_convert_fusion
  1366.9 0.0 reduce-scatter.2.cloned.1.call-update
  1366.9 81.8 %reduce-scatter.2.cloned.1.call-done = bf16[512,1024]{1,0:T(8,128)(2,1)} async-done(((bf16[512,4096]{1,0:T(8,128)(2,1)}), bf16[512,1024]{1,0:T(8,128)(2,1)}) %reduce-scatter.2.cloned.1.call-update) | async-done | bytes 1048592 | tf_op jit(solution)/shard_map/reduce_scatter | solution.py:55
  (18 shorter events, 0.2 us)
Async XLA Ops:
  7.2 120.5 %all-gather.2.cloned.1.call-start = ((), (), s32[]{:S(2)}) async-start(), calls=%async_computation.1 | async-start | bytes 8519680 | tf_op jit(solution)/shard_map/all_gather | solution.py:43
  7.9 1440.8 %reduce-scatter.2.cloned.1.call-start = ((), (), s32[]{:S(2)}) async-start(), calls=%async_computation.2 | async-start | bytes 5242880 | tf_op jit(solution)/shard_map/reduce_scatter | solution.py:55
  127.7 5.8 copy-start
  1057.3 143.3 %copy-start.2 = (f32[512]{0:T(512)}, f32[512]{0:T(512)S(1)}, u32[]{:S(2)}) copy-start(f32[512]{0:T(512)S(1)} %subtract_multiply_fusion.14) | copy-start | bytes 6148
  1339.1 18.2 %copy-start.1 = (f32[1024]{0:T(1024)}, f32[1024]{0:T(1024)S(1)}, u32[]{:S(2)}) copy-start(f32[1024]{0:T(1024)S(1)} %subtract_multiply_fusion.10) | copy-start | bytes 12292
Sparse Core Ops, SparseCore 0:
  9.9 117.7 all-gather.1
  1367.1 81.5 reduce-scatter.1
where the time goes:
time: 1460 us
  blocking collectives  1210 us (83%)
  waiting for transfers between devices  199 us (14%)
  matrix products  16.5 us (1%)
  other arithmetic  15.6 us (1%)
    pmax x4, blocking collectives, col_lse(): top = lax.pmax(local_max, 'rows')  569 us
    psum x4, blocking collectives, col_lse(): total = lax.psum(local_sum * jnp.exp(local_max - top), 'rows')  554 us
    all_gather x1, waiting for transfers between devices, per_device(): whole = lax.all_gather(data, 'rows', axis=1, tiled=True)  117 us
    reduce_scatter x1, waiting for transfers between devices, per_device(): lax.psum_scatter(partial_targets.astype(jnp.bfloat16), 'cols', scatter_di...  81.8 us
    psum x5, blocking collectives, row_lse(): total = lax.psum(local_sum * jnp.exp(local_max - top), 'cols')  44.3 us
    pmax x5, blocking collectives, row_lse(): top = lax.pmax(local_max, 'cols')  42.2 us
  transfers between devices with their start and end apart: 2, of which 2 were waited for; matrix products, arithmetic and copies ran while one was open for 0% of the time, Pallas kernels for 0%

commit v1 on v0

v1 whole, which is shorter than its diff:
```python
import functools
import math

import jax
import jax.numpy as jnp
from jax import lax
from jax.experimental import pallas as pl
from jax.experimental.pallas import tpu as pltpu
from jax.sharding import PartitionSpec as P

ITERS = 4
EPSILON = 0.05
SCALE_BITS = 64.0
SCALE = 2.0**64
MESH = pl.DeviceIdType.MESH
F32 = jnp.float32
BF16 = jnp.bfloat16


def kernel(
    noise_ref, data_ref, out_ref, row_ref, col_ref,
    whole, scores, mass, weights, rmsg, rbuf, cmsg, cbuf,
    gsend, grecv, bsend, brecv, rsend, rrecv, csend, crecv,
):
    rows_total = 32768
    cols_total = 4096
    width = 4096
    to_log2 = 1.0 / (EPSILON * math.log(2.0))
    me = lax.axis_index("rows")
    zh = lax.axis_index("cols")
    y, x, zl, core = me // 16, (me // 4) % 4, (me // 2) % 2, me % 2

    def index(yy, xx, ll):
        return ((((yy + 4) % 4) * 4 + (xx + 4) % 4) * 2 + ll) * 2 + core

    barrier = pltpu.get_barrier_semaphore()

    def greet(o, carry):
        pl.semaphore_signal(barrier, inc=1, device_id=((me + o) % 64, zh), device_id_type=MESH)
        return carry

    lax.fori_loop(1, 64, greet, 0)
    for o in range(1, 4):
        pl.semaphore_signal(barrier, inc=1, device_id=(me, (zh + o) % 4), device_id_type=MESH)

    eye = (
        lax.broadcasted_iota(jnp.int32, (64, 64), 0) == lax.broadcasted_iota(jnp.int32, (64, 64), 1)
    ).astype(F32).astype(BF16)
    whole[me] = lax.dot_general(
        eye, data_ref[...], (((1,), (1,)), ((), ())), preferred_element_type=F32
    ).astype(BF16)
    pl.semaphore_wait(barrier, 66)

    sends = []

    def move(t, slot, target, half=None):
        ref = whole.at[slot] if half is None else whole.at[slot, pl.ds(half * 32, 32)]
        copy = pltpu.make_async_remote_copy(
            src_ref=ref, dst_ref=ref, send_sem=gsend.at[t], recv_sem=grecv.at[t],
            device_id=(target, zh), device_id_type=MESH,
        )
        copy.start()
        sends.append(copy)

    def arrived(t, slot, half=None):
        ref = whole.at[slot] if half is None else whole.at[slot, pl.ds(half * 32, 32)]
        pltpu.make_async_remote_copy(
            src_ref=ref, dst_ref=ref, send_sem=gsend.at[t], recv_sem=grecv.at[t],
            device_id=(me, zh), device_id_type=MESH,
        ).wait_recv()

    sibling = me + 1 - 2 * core
    shared = []

    def share(slot):
        t = len(shared)
        copy = pltpu.make_async_remote_copy(
            src_ref=whole.at[slot], dst_ref=whole.at[slot], send_sem=bsend.at[t],
            recv_sem=brecv.at[t], device_id=(sibling, zh), device_id_type=MESH,
        )
        copy.start()
        shared.append((copy, slot + 1 - 2 * core))

    move(0, me, index(y, x, 1 - zl))
    share(me)
    arrived(0, index(y, x, 1 - zl))
    share(index(y, x, 1 - zl))

    def at(part, da, db):
        return index(y + db, x + da, 0) if part == 0 else index(y + da, x + db, 1)

    def near(part, da, db):
        return index(y + db, x + da, zl) if part == 0 else index(y + da, x + db, zl)

    base = (1, 25)
    second = ((0, 0), (-1, 3), (1, 6), (2, 9))
    for part in (0, 1):
        b = base[part]
        move(b + 0, at(part, 0, 0), near(part, 1, 0))
        move(b + 1, at(part, 0, 0), near(part, -1, 0))

    def along_second(part, da, n):
        b = base[part] + 4 + 5 * n
        move(b + 0, at(part, da, 0), near(part, 0, 1))
        move(b + 1, at(part, da, 0), near(part, 0, -1))

    for part in (0, 1):
        along_second(part, 0, 0)
    for part in (0, 1):
        b = base[part]
        arrived(b + 0, at(part, -1, 0))
        move(b + 2, at(part, -1, 0), near(part, 1, 0), 0)
        arrived(b + 1, at(part, 1, 0))
        move(b + 3, at(part, 1, 0), near(part, -1, 0), 1)
    for part in (0, 1):
        along_second(part, -1, 1)
        share(at(part, -1, 0))
        along_second(part, 1, 2)
        share(at(part, 1, 0))

    def relay(part, da, n, up):
        b = base[part] + 4 + 5 * n
        arrived(b + 0, at(part, da, -1))
        if up:
            move(b + 2, at(part, da, -1), near(part, 0, 1))
        share(at(part, da, -1))
        arrived(b + 1, at(part, da, 1))
        if not up:
            move(b + 2, at(part, da, 1), near(part, 0, -1))
        share(at(part, da, 1))

    for part in (0, 1):
        relay(part, 0, 0, True)
    for part in (0, 1):
        b = base[part]
        arrived(b + 2, at(part, 2, 0), 0)
        arrived(b + 3, at(part, 2, 0), 1)
        along_second(part, 2, 3)
        share(at(part, 2, 0))
    for part in (0, 1):
        relay(part, -1, 1, False)
        relay(part, 1, 2, True)
    for part in (0, 1):
        relay(part, 2, 3, False)
    for n, da in enumerate((0, -1, 1, 2)):
        for part in (0, 1):
            b = base[part] + 4 + 5 * n
            arrived(b + 2, at(part, da, 2))
            share(at(part, da, 2))
    for copy in sends:
        copy.wait_send()
    for copy, slot in shared:
        copy.wait_send()
        copy.wait_recv()

    factor = 2.0 * to_log2 / width

    @pl.loop(0, 4)
    def _(n):
        cols = pl.ds(pl.multiple_of(n * 256, 256), 256)
        right = whole[:, :, cols].reshape(4096, 256)
        scores[:, cols] = factor * jnp.dot(noise_ref[...], right, preferred_element_type=F32)

    def square_cols(i, acc):
        v = whole[i].astype(F32)
        v = v * v
        return acc + jnp.sum(v.reshape(8, 8, 1024), axis=0)

    data_sq = jnp.sum(lax.fori_loop(0, 64, square_cols, jnp.zeros((8, 1024), F32)), axis=0, keepdims=True)

    diagonal = lax.broadcasted_iota(jnp.int32, (128, 128), 0) == lax.broadcasted_iota(jnp.int32, (128, 128), 1)

    def compact(column):
        parts = [
            jnp.sum(jnp.where(diagonal, column[i * 128:(i + 1) * 128], 0.0), axis=0, keepdims=True)
            for i in range(4)
        ]
        return jnp.concatenate(parts + parts, axis=0)

    def spread(packed):
        parts = [
            jnp.sum(jnp.where(diagonal, packed[i:i + 1], 0.0), axis=1, keepdims=True)
            for i in range(4)
        ]
        return jnp.concatenate(parts, axis=0)

    def fold(line):
        return jnp.concatenate([line[:, i * 128:(i + 1) * 128] for i in range(8)], axis=0)

    def unfold(packed):
        return jnp.concatenate([packed[i:i + 1] for i in range(8)], axis=1)

    def exchange_rows(e, packed):
        rmsg[e] = packed
        for o in range(1, 4):
            pltpu.make_async_remote_copy(
                src_ref=rmsg.at[e], dst_ref=rbuf.at[e, o - 1], send_sem=rsend.at[e, o - 1],
                recv_sem=rrecv.at[e, o - 1], device_id=(me, (zh + o) % 4), device_id_type=MESH,
            ).start()
        for o in range(1, 4):
            pltpu.make_async_remote_copy(
                src_ref=rmsg.at[e], dst_ref=rbuf.at[e, o - 1], send_sem=rsend.at[e, o - 1],
                recv_sem=rrecv.at[e, o - 1], device_id=(me, (zh + o) % 4), device_id_type=MESH,
            ).wait()
        return rbuf[e]

    def exchange_cols(e, packed):
        cmsg[e] = packed

        def start(o, carry):
            pltpu.make_async_remote_copy(
                src_ref=cmsg.at[e], dst_ref=cbuf.at[e, o - 1], send_sem=csend.at[e],
                recv_sem=crecv.at[e], device_id=((me + o) % 64, zh), device_id_type=MESH,
            ).start()
            return carry

        lax.fori_loop(1, 64, start, 0)
        everything = pltpu.make_async_remote_copy(
            src_ref=cbuf.at[e], dst_ref=cbuf.at[e], send_sem=csend.at[e],
            recv_sem=crecv.at[e], device_id=(sibling, zh), device_id_type=MESH,
        )
        everything.wait_recv()
        everything.wait_send()
        return cbuf[e]

    def combine(own, others):
        top = jnp.maximum(own, jnp.max(others, axis=0))
        total = jnp.exp2(own - top) + jnp.sum(jnp.exp2(others - top[None]), axis=0)
        return top + jnp.log2(total)

    log_rows = -math.log2(rows_total)
    log_cols = -math.log2(cols_total)

    start_cols = data_sq * (-to_log2 / width)
    logits = scores[...] + start_cols
    top = jnp.max(logits, axis=1, keepdims=True)
    own = compact(top + jnp.log2(jnp.sum(jnp.exp2(logits - top), axis=1, keepdims=True)))
    row_pot = log_rows - combine(own, exchange_rows(0, own))
    logits = scores[...] + spread(row_pot)
    top = jnp.max(logits, axis=0, keepdims=True)
    own = fold(top + jnp.log2(jnp.sum(jnp.exp2(logits - top), axis=0, keepdims=True)))
    col_pot = log_cols - combine(own, exchange_cols(0, own))
    mass[...] = jnp.exp2(scores[...] + (spread(row_pot) + SCALE_BITS) + unfold(col_pot))

    right_scale = jnp.ones((8, 128), F32)
    for e in range(1, ITERS):
        own = compact(jnp.sum(mass[...] * unfold(right_scale), axis=1, keepdims=True))
        total = own + jnp.sum(exchange_rows(e, own), axis=0)
        left_scale = (SCALE / rows_total) / total
        own = fold(jnp.sum(mass[...] * spread(left_scale), axis=0, keepdims=True))
        total = own + jnp.sum(exchange_cols(e, own), axis=0)
        right_scale = (SCALE / cols_total) / total

    row_log = row_pot + jnp.log2(left_scale)
    col_log = col_pot + jnp.log2(right_scale)

    v = noise_ref[...].astype(F32)
    noise_sq = compact(jnp.sum(v * v, axis=1, keepdims=True))
    row_ref[...] = row_log * (1.0 / to_log2) + noise_sq * (1.0 / width)
    col_ref[...] = col_log * (1.0 / to_log2) + fold(data_sq) * (1.0 / width)

    plan = mass[...] * unfold(right_scale)
    own = compact(jnp.sum(plan, axis=1, keepdims=True))
    total = own + jnp.sum(exchange_rows(ITERS, own), axis=0)
    weights[...] = (plan * spread(1.0 / total)).astype(BF16)

    @pl.loop(0, 8)
    def _(n):
        right = whole[pl.ds(n * 8, 8)].reshape(512, 1024)
        cols = pl.ds(pl.multiple_of(n * 512, 512), 512)
        out_ref[:, cols] = lax.dot_general(
            weights[...], right, (((1,), (1,)), ((), ())), preferred_element_type=F32
        ).astype(BF16)


def per_device(noise, data):
    vmem = pl.BlockSpec(memory_space=pltpu.VMEM)
    dma = pltpu.SemaphoreType.DMA
    partial, row_pot, col_pot = pl.pallas_call(
        kernel,
        out_shape=(
            jax.ShapeDtypeStruct((512, 4096), BF16),
            jax.ShapeDtypeStruct((8, 128), F32),
            jax.ShapeDtypeStruct((8, 128), F32),
        ),
        in_specs=[vmem, vmem],
        out_specs=(vmem, vmem, vmem),
        scratch_shapes=[
            pltpu.VMEM((64, 64, 1024), BF16),
            pltpu.VMEM((512, 1024), F32),
            pltpu.VMEM((512, 1024), F32),
            pltpu.VMEM((512, 1024), BF16),
            pltpu.VMEM((ITERS + 1, 8, 128), F32),
            pltpu.VMEM((ITERS + 1, 3, 8, 128), F32),
            pltpu.VMEM((ITERS, 8, 128), F32),
            pltpu.VMEM((ITERS, 63, 8, 128), F32),
            dma((49,)),
            dma((49,)),
            dma((32,)),
            dma((32,)),
            dma((ITERS + 1, 3)),
            dma((ITERS + 1, 3)),
            dma((ITERS,)),
            dma((ITERS,)),
        ],
        compiler_params=pltpu.CompilerParams(
            collective_id=0, has_side_effects=True, vmem_limit_bytes=56 * 2**20
        ),
        cost_estimate=pl.CostEstimate(flops=9 * 10**9, bytes_accessed=9 * 2**20, transcendentals=3 * 10**6),
    )(noise, data)
    targets = lax.psum_scatter(partial, "cols", scatter_dimension=1, tiled=True)
    return targets, row_pot[:4].reshape(512), col_pot.reshape(1024)


def solution(mesh):
    in_specs = (P("rows", None), P("cols", "rows"))
    out_specs = (P("rows", "cols"), P("rows"), P("cols"))
    return jax.shard_map(
        per_device, mesh=mesh, in_specs=in_specs, out_specs=out_specs, check_vma=False
    )
```

time: 1460 us -> 208 us (0.14)
  blocking collectives: 1210 us -> 0 us
  waiting for transfers between devices: 199 us -> 79.9 us
  Pallas kernels: 0 us -> 111 us
  matrix products: 16.5 us -> 0 us
  other arithmetic: 15.6 us -> 0 us
    pmax x9 -> x0, blocking collectives: 612 us -> none  [the longest x4 569 us: col_lse(): top = lax.pmax(local_max, 'rows')]
    psum x9 -> x0, blocking collectives: 598 us -> none  [the longest x4 554 us: col_lse(): total = lax.psum(local_sum * jnp.exp(local_max - top), 'rows')]
    all_gather x1 -> x0, waiting for transfers between devices: 117 us -> none  [per_device(): whole = lax.all_gather(data, 'rows', axis=1, tiled=True)]
    pallas_call x0 -> x1, Pallas kernels: none -> 111 us  [per_device(): pl.pallas_call(kernel, out_shape=(jax.ShapeDtypeStruct((512, 4096), BF16)...]
    dot_general x2 -> x0, matrix products: 16.5 us -> none  [the longest x1 9.63 us: per_device(): jnp.dot(weights, whole, preferred_element_type=jnp.float32)]
  transfers between devices with their start and end apart: 2 -> 1, of which waited for: 2 -> 1; matrix products, arithmetic and copies ran while one was open for 0% -> 0% of each run, Pallas kernels for 0% -> 0%
where the time goes in v1:
time: 208 us
  Pallas kernels  111 us (53%)
  waiting for transfers between devices  79.9 us (38%)
  between operations  14.1 us (7%)
  local copies, waits for them, and re-layouts  3.55 us (2%)
    pallas_call x1, Pallas kernels, per_device(): pl.pallas_call(kernel, out_shape=(jax.ShapeDtypeStruct((512, 4096), BF16)...  111 us
    reduce_scatter x1, waiting for transfers between devices, per_device(): targets = lax.psum_scatter(partial, 'cols', scatter_dimension=1, tiled=True)  79.9 us
  transfers between devices with their start and end apart: 1, of which 1 were waited for; matrix products, arithmetic and copies ran while one was open for 0% of the time, Pallas kernels for 0%

profile of v1, /device:TPU:1, one launch (start us, length us, event | category | flops | bytes accessed | tf_op | source)
XLA Modules:
  0.0 208.3 jit_solution(12824600348016814888)
XLA Ops:
  7.2 0.0 reduce-scatter.2.cloned.1.call-start
  7.2 1.7 copy.5.data_ref
  9.0 110.8 %shard_map.49 = (bf16[512,4096]{1,0:T(8,128)(2,1)}, f32[8,128]{1,0:T(8,128)}, f32[8,128]{1,0:T(8,128)}) custom-call(bf16[512,4096]{1,0:T(8,128)(2,1)} %noise_ref.1, bf16[1024,64]{1,0:T(8,128)(2,1)} %copy.5.data_ref), custom_call_target="tpu_custom_call" | custom-call | flops 8999999488 | bytes 9437184 | tf_op jit(solution)/shard_map/pallas_call | solution.py:279
  119.7 0.0 copy-start.1
  119.7 0.0 copy-start
  119.8 0.0 reduce-scatter.2.cloned.1.call-update
  119.8 0.6 copy-done.1
  120.4 0.6 slice_bitcast_fusion
  121.0 79.9 %reduce-scatter.2.cloned.1.call-done = bf16[512,1024]{1,0:T(8,128)(2,1)} async-done(((bf16[512,4096]{1,0:T(8,128)(2,1)}), bf16[512,1024]{1,0:T(8,128)(2,1)}) %reduce-scatter.2.cloned.1.call-update) | async-done | bytes 1048592 | tf_op jit(solution)/shard_map/reduce_scatter | solution.py:311
  200.9 0.0 copy-done
  200.9 0.6 copy.7
Async XLA Ops:
  7.2 193.7 %reduce-scatter.2.cloned.1.call-start = ((), (), s32[]{:S(2)}) async-start(), calls=%async_computation.1 | async-start | bytes 5242880 | tf_op jit(solution)/shard_map/reduce_scatter | solution.py:311
  119.7 0.7 copy-start.1
  119.7 81.2 %copy-start = (f32[8,128]{1,0:T(8,128)S(1)}, f32[8,128]{1,0:T(8,128)}, u32[]{:S(2)}) copy-start(f32[8,128]{1,0:T(8,128)} %get-tuple-element.8) | copy-start | bytes 12292
Sparse Core Ops, SparseCore 0:
  119.9 80.9 reduce-scatter.1

commit v2 on v1

v2 whole, which is shorter than its diff:
```python
import functools
import math

import jax
import jax.numpy as jnp
from jax import lax
from jax.experimental import pallas as pl
from jax.experimental.pallas import tpu as pltpu
from jax.sharding import PartitionSpec as P

ITERS = 4
EPSILON = 0.05
SCALE_BITS = 64.0
SCALE = 2.0**64
MESH = pl.DeviceIdType.MESH
F32 = jnp.float32
BF16 = jnp.bfloat16


def kernel(
    noise_hbm, data_ref, out_ref, row_ref, col_ref,
    noise_ref, whole_a, whole_b, scores, mass, plan_ref, part_ref, got_ref, own_ref,
    rmsg, rbuf, cmsg, cbuf, pmsg, pbuf,
    nsem, zsend, zrecv, asems, bsems, rsend, rrecv, csend, crecv, psend, precv, tsend, trecv,
):
    rows_total = 32768
    cols_total = 4096
    width = 4096
    to_log2 = 1.0 / (EPSILON * math.log(2.0))
    factor = 2.0 * to_log2 / width
    me = lax.axis_index("rows")
    zh = lax.axis_index("cols")
    y, x, zl, core = me // 16, (me // 4) % 4, (me // 2) % 2, me % 2
    sibling = me + 1 - 2 * core

    def index(yy, xx, ll):
        return ((((yy + 4) % 4) * 4 + (xx + 4) % 4) * 2 + ll) * 2 + core

    load = pltpu.make_async_copy(noise_hbm, noise_ref, nsem)
    load.start()

    barrier = pltpu.get_barrier_semaphore()

    def greet(o, carry):
        pl.semaphore_signal(barrier, inc=1, device_id=((me + o) % 64, zh), device_id_type=MESH)
        return carry

    lax.fori_loop(1, 64, greet, 0)
    for o in range(1, 4):
        pl.semaphore_signal(barrier, inc=1, device_id=(me, (zh + o) % 4), device_id_type=MESH)
    whole_a[me] = data_ref[...]
    pl.semaphore_wait(barrier, 66)

    def at(part, da, db):
        return index(y + db, x + da, 0) if part == 0 else index(y + da, x + db, 1)

    def near(part, da, db):
        return index(y + db, x + da, zl) if part == 0 else index(y + da, x + db, zl)

    base = (1, 25)
    turns = (0, -1, 1, 2)

    class Gather:
        def __init__(self, whole, sems):
            self.whole = whole
            self.gsend, self.grecv, self.bsend, self.brecv = sems
            self.sent = []
            self.shared = 0
            self.of_turn = {n: [] for n in range(4)}

        def remote(self, slot, half, send, recv, target):
            ref = self.whole.at[slot] if half is None else self.whole.at[slot, pl.ds(half * 32, 32)]
            return pltpu.make_async_remote_copy(
                src_ref=ref, dst_ref=ref, send_sem=send, recv_sem=recv,
                device_id=(target, zh), device_id_type=MESH,
            )

        def move(self, t, slot, target, half=None):
            copy = self.remote(slot, half, self.gsend.at[t], self.grecv.at[t], target)
            copy.start()
            self.sent.append(copy)

        def arrived(self, t, slot, half=None):
            self.remote(slot, half, self.gsend.at[t], self.grecv.at[t], sibling).wait_recv()

        def share(self, slot, n):
            t = self.shared
            self.shared += 1
            copy = self.remote(slot, None, self.bsend.at[t], self.brecv.at[t], sibling)
            copy.start()
            self.sent.append(copy)
            theirs = slot + 1 - 2 * core
            self.of_turn[n].append(self.remote(theirs, None, self.bsend.at[t], self.brecv.at[t], sibling))

        def begin(self):
            self.move(0, me, index(y, x, 1 - zl))
            self.share(me, 0)

        def first(self):
            self.arrived(0, index(y, x, 1 - zl))
            for part in (0, 1):
                b = base[part]
                self.move(b + 0, at(part, 0, 0), near(part, 1, 0))
                self.move(b + 1, at(part, 0, 0), near(part, -1, 0))
            self.share(index(y, x, 1 - zl), 0)

        def second(self, n):
            for part in (0, 1):
                b = base[part] + 4 + 5 * n
                self.move(b + 0, at(part, turns[n], 0), near(part, 0, 1))
                self.move(b + 1, at(part, turns[n], 0), near(part, 0, -1))

        def halves(self):
            for part in (0, 1):
                b = base[part]
                self.arrived(b + 0, at(part, -1, 0))
                self.move(b + 2, at(part, -1, 0), near(part, 1, 0), 0)
                self.arrived(b + 1, at(part, 1, 0))
                self.move(b + 3, at(part, 1, 0), near(part, -1, 0), 1)

        def share_first(self):
            for part in (0, 1):
                self.share(at(part, -1, 0), 1)
                self.share(at(part, 1, 0), 2)

        def opposite(self):
            for part in (0, 1):
                b = base[part]
                self.arrived(b + 2, at(part, 2, 0), 0)
                self.arrived(b + 3, at(part, 2, 0), 1)
                self.share(at(part, 2, 0), 3)

        def relay(self, n, up):
            for part in (0, 1):
                b = base[part] + 4 + 5 * n
                self.arrived(b + 0, at(part, turns[n], -1))
                if up:
                    self.move(b + 2, at(part, turns[n], -1), near(part, 0, 1))
                self.share(at(part, turns[n], -1), n)
                self.arrived(b + 1, at(part, turns[n], 1))
                if not up:
                    self.move(b + 2, at(part, turns[n], 1), near(part, 0, -1))
                self.share(at(part, turns[n], 1), n)

        def last(self, n):
            for part in (0, 1):
                self.arrived(base[part] + 4 + 5 * n + 2, at(part, turns[n], 2))
                self.share(at(part, turns[n], 2), n)

        def turn_done(self, n):
            for copy in self.of_turn[n]:
                copy.wait_recv()

        def done(self):
            for copy in self.sent:
                copy.wait_send()

    def add_gram(whole, n, keep):
        for part in (0, 1):
            firsts = [
                (((i * 4 + (x + turns[n] + 4) % 4) * 2 + part) * 2) if part == 0
                else (((((y + turns[n] + 4) % 4) * 4 + i) * 2 + part) * 2)
                for i in range(4)
            ]
            left = jnp.concatenate(
                [noise_ref[:, pl.ds(pl.multiple_of(f * 64, 128), 128)] for f in firsts], axis=1
            )
            for c in range(4):
                cols = pl.ds(c * 256, 256)
                right = jnp.concatenate(
                    [whole[pl.ds(f, 2), :, cols].reshape(128, 256) for f in firsts], axis=0
                )
                value = factor * jnp.dot(left, right, preferred_element_type=F32)
                scores[:, cols] = value if n == 0 and part == 0 else scores[:, cols] + value

    first_block = Gather(whole_a, [asems.at[i] for i in range(4)])
    other_block = Gather(whole_b, [bsems.at[i] for i in range(4)])

    first_block.begin()
    across = pltpu.make_async_remote_copy(
        src_ref=whole_a.at[me], dst_ref=whole_b.at[me], send_sem=zsend, recv_sem=zrecv,
        device_id=(me, (zh + 2) % 4), device_id_type=MESH,
    )
    first_block.first()
    across.start()
    first_block.second(0)
    first_block.halves()
    first_block.second(1)
    first_block.second(2)
    first_block.share_first()
    first_block.relay(0, True)
    first_block.opposite()
    first_block.second(3)
    first_block.relay(1, False)
    first_block.relay(2, True)
    first_block.last(0)
    first_block.relay(3, False)
    load.wait()
    first_block.turn_done(0)
    add_gram(whole_a, 0, False)
    for n in (1, 2, 3):
        first_block.last(n)
        first_block.turn_done(n)
        add_gram(whole_a, n, False)

    def square_cols(i, acc):
        v = whole_a[i].astype(F32)
        v = v * v
        return acc + jnp.sum(v.reshape(8, 8, 1024), axis=0)

    data_sq = jnp.sum(lax.fori_loop(0, 64, square_cols, jnp.zeros((8, 1024), F32)), axis=0, keepdims=True)
    diagonal = lax.broadcasted_iota(jnp.int32, (128, 128), 0) == lax.broadcasted_iota(jnp.int32, (128, 128), 1)

    def compact(column):
        parts = [
            jnp.sum(jnp.where(diagonal, column[i * 128:(i + 1) * 128], 0.0), axis=0, keepdims=True)
            for i in range(4)
        ]
        return jnp.concatenate(parts + parts, axis=0)

    def spread(packed):
        parts = [
            jnp.sum(jnp.where(diagonal, packed[i:i + 1], 0.0), axis=1, keepdims=True)
            for i in range(4)
        ]
        return jnp.concatenate(parts, axis=0)

    def fold(line):
        return jnp.concatenate([line[:, i * 128:(i + 1) * 128] for i in range(8)], axis=0)

    def unfold(packed):
        return jnp.concatenate([packed[i:i + 1] for i in range(8)], axis=1)

    def exchange_rows(e, packed, between):
        rmsg[e] = packed
        copies = [
            pltpu.make_async_remote_copy(
                src_ref=rmsg.at[e], dst_ref=rbuf.at[e, o - 1], send_sem=rsend.at[e, o - 1],
                recv_sem=rrecv.at[e, o - 1], device_id=(me, (zh + o) % 4), device_id_type=MESH,
            )
            for o in range(1, 4)
        ]
        for copy in copies:
            copy.start()
        between()
        for copy in copies:
            copy.wait()
        return rbuf[e]

    def exchange_cols(e, packed, between):
        cmsg[e] = packed

        def start(o, carry):
            pltpu.make_async_remote_copy(
                src_ref=cmsg.at[e], dst_ref=cbuf.at[e, o - 1], send_sem=csend.at[e],
                recv_sem=crecv.at[e], device_id=((me + o) % 64, zh), device_id_type=MESH,
            ).start()
            return carry

        lax.fori_loop(1, 64, start, 0)
        between()
        everything = pltpu.make_async_remote_copy(
            src_ref=cbuf.at[e], dst_ref=cbuf.at[e], send_sem=csend.at[e],
            recv_sem=crecv.at[e], device_id=(sibling, zh), device_id_type=MESH,
        )
        everything.wait_recv()
        everything.wait_send()
        return cbuf[e]

    def step_r1():
        across.wait()
        other_block.begin()

    def step_c1():
        other_block.first()

    def step_r2():
        other_block.halves()
        other_block.second(0)
        other_block.share_first()

    def step_c2():
        other_block.second(1)
        other_block.opposite()

    def step_r3():
        other_block.second(2)

    def step_c3():
        other_block.relay(0, True)
        other_block.second(3)

    def step_r4():
        other_block.relay(1, False)
        other_block.relay(2, True)
        other_block.last(0)

    def step_c4():
        other_block.relay(3, False)

    row_steps = (step_r1, step_r2, step_r3, step_r4)
    col_steps = (step_c1, step_c2, step_c3, step_c4)

    def combine(own, others):
        top = jnp.maximum(own, jnp.max(others, axis=0))
        total = jnp.exp2(own - top) + jnp.sum(jnp.exp2(others - top[None]), axis=0)
        return top + jnp.log2(total)

    log_rows = -math.log2(rows_total)
    log_cols = -math.log2(cols_total)

    start_cols = data_sq * (-to_log2 / width)
    logits = scores[...] + start_cols
    top = jnp.max(logits, axis=1, keepdims=True)
    own = compact(top + jnp.log2(jnp.sum(jnp.exp2(logits - top), axis=1, keepdims=True)))
    row_pot = log_rows - combine(own, exchange_rows(0, own, row_steps[0]))
    logits = scores[...] + spread(row_pot)
    top = jnp.max(logits, axis=0, keepdims=True)
    own = fold(top + jnp.log2(jnp.sum(jnp.exp2(logits - top), axis=0, keepdims=True)))
    col_pot = log_cols - combine(own, exchange_cols(0, own, col_steps[0]))
    mass[...] = jnp.exp2(scores[...] + (spread(row_pot) + SCALE_BITS) + unfold(col_pot))

    right_scale = jnp.ones((8, 128), F32)
    for e in range(1, ITERS):
        own = compact(jnp.sum(mass[...] * unfold(right_scale), axis=1, keepdims=True))
        total = own + jnp.sum(exchange_rows(e, own, row_steps[e]), axis=0)
        left_scale = (SCALE / rows_total) / total
        own = fold(jnp.sum(mass[...] * spread(left_scale), axis=0, keepdims=True))
        total = own + jnp.sum(exchange_cols(e, own, col_steps[e]), axis=0)
        right_scale = (SCALE / cols_total) / total

    row_log = row_pot + jnp.log2(left_scale)
    col_log = col_pot + jnp.log2(right_scale)

    pmsg[0] = col_log
    swap = pltpu.make_async_remote_copy(
        src_ref=pmsg.at[0], dst_ref=pbuf.at[0], send_sem=psend.at[0], recv_sem=precv.at[0],
        device_id=(me, (zh + 2) % 4), device_id_type=MESH,
    )
    swap.start()
    row_bits = spread(row_log)
    plan = jnp.exp2(scores[...] + row_bits + unfold(col_log))
    plan_ref[:, :1024] = plan.astype(BF16)
    sums = jnp.sum(plan, axis=1, keepdims=True)

    other_block.turn_done(0)
    add_gram(whole_b, 0, False)
    for n in (1, 2, 3):
        other_block.last(n)
        other_block.turn_done(n)
        add_gram(whole_b, n, False)
    swap.wait()
    plan = jnp.exp2(scores[...] + row_bits + unfold(pbuf[0]))
    plan_ref[:, 1024:] = plan.astype(BF16)
    sums = compact(sums + jnp.sum(plan, axis=1, keepdims=True))
    pmsg[1] = sums
    tell = pltpu.make_async_remote_copy(
        src_ref=pmsg.at[1], dst_ref=pbuf.at[1], send_sem=psend.at[1], recv_sem=precv.at[1],
        device_id=(me, (zh + 1) % 4), device_id_type=MESH,
    )
    tell.start()

    def product(rows, q, c):
        total = None
        for half, whole in ((0, whole_a), (1, whole_b)):
            right = whole[pl.ds(q * 16 + c * 4, 4)].reshape(256, 1024)
            value = lax.dot_general(
                plan_ref[rows, pl.ds(half * 1024, 1024)], right, (((1,), (1,)), ((), ())),
                preferred_element_type=F32,
            )
            total = value if total is None else total + value
        return total

    hand = []
    for c in range(4):
        for d, step in ((0, 1), (1, 3)):
            q = (zh + step) % 4
            part_ref[d, c] = product(pl.ds(d * 256, 256), q, c).astype(BF16)
            copy = pltpu.make_async_remote_copy(
                src_ref=part_ref.at[d, c], dst_ref=got_ref.at[d, c], send_sem=tsend.at[d, c],
                recv_sem=trecv.at[d, c], device_id=(me, q), device_id_type=MESH,
            )
            copy.start()
            hand.append(copy)
    for c in range(4):
        own_ref[:, pl.ds(c * 256, 256)] = product(pl.ds(0, 512), zh, c)

    v = noise_ref[...].astype(F32)
    noise_sq = compact(jnp.sum(v * v, axis=1, keepdims=True))
    row_ref[...] = row_log * (1.0 / to_log2) + noise_sq * (1.0 / width)
    col_ref[...] = col_log * (1.0 / to_log2) + fold(data_sq) * (1.0 / width)

    tell.wait()
    inverse = spread(1.0 / (sums + pbuf[1]))
    for c in range(4):
        for d in (0, 1):
            hand[c * 2 + d].wait_recv()
            rows, cols = pl.ds(d * 256, 256), pl.ds(c * 256, 256)
            value = own_ref[rows, cols] + got_ref[d, c].astype(F32)
            out_ref[rows, cols] = (value * inverse[d * 256:(d + 1) * 256]).astype(BF16)
    for copy in hand:
        copy.wait_send()
    first_block.done()
    other_block.done()


def per_device(noise, data):
    vmem = pl.BlockSpec(memory_space=pltpu.VMEM)
    dma = pltpu.SemaphoreType.DMA
    targets, row_pot, col_pot = pl.pallas_call(
        kernel,
        out_shape=(
            jax.ShapeDtypeStruct((512, 1024), BF16),
            jax.ShapeDtypeStruct((8, 128), F32),
            jax.ShapeDtypeStruct((8, 128), F32),
        ),
        in_specs=[pl.BlockSpec(memory_space=pl.ANY), vmem],
        out_specs=(vmem, vmem, vmem),
        scratch_shapes=[
            pltpu.VMEM((512, 4096), BF16),
            pltpu.VMEM((64, 64, 1024), BF16),
            pltpu.VMEM((64, 64, 1024), BF16),
            pltpu.VMEM((512, 1024), F32),
            pltpu.VMEM((512, 1024), F32),
            pltpu.VMEM((512, 2048), BF16),
            pltpu.VMEM((2, 4, 256, 256), BF16),
            pltpu.VMEM((2, 4, 256, 256), BF16),
            pltpu.VMEM((512, 1024), F32),
            pltpu.VMEM((ITERS, 8, 128), F32),
            pltpu.VMEM((ITERS, 3, 8, 128), F32),
            pltpu.VMEM((ITERS, 8, 128), F32),
            pltpu.VMEM((ITERS, 63, 8, 128), F32),
            pltpu.VMEM((2, 8, 128), F32),
            pltpu.VMEM((2, 8, 128), F32),
            dma,
            dma,
            dma,
            dma((4, 49)),
            dma((4, 49)),
            dma((ITERS, 3)),
            dma((ITERS, 3)),
            dma((ITERS,)),
            dma((ITERS,)),
            dma((2,)),
            dma((2,)),
            dma((2, 4)),
            dma((2, 4)),
        ],
        compiler_params=pltpu.CompilerParams(
            collective_id=0, has_side_effects=True, vmem_limit_bytes=58 * 2**20
        ),
        cost_estimate=pl.CostEstimate(flops=18 * 10**9, bytes_accessed=9 * 2**20, transcendentals=3 * 10**6),
    )(noise, data.T)
    return targets, row_pot[:4].reshape(512), col_pot.reshape(1024)


def solution(mesh):
    in_specs = (P("rows", None), P("cols", "rows"))
    out_specs = (P("rows", "cols"), P("rows"), P("cols"))
    return jax.shard_map(
        per_device, mesh=mesh, in_specs=in_specs, out_specs=out_specs, check_vma=False
    )
```

time: 208 us -> 143 us (0.69)
  waiting for transfers between devices: 79.9 us -> 0 us
  Pallas kernels: 111 us -> 137 us
  between operations: 14.1 us -> 0.64 us
    reduce_scatter x1 -> x0, waiting for transfers between devices: 79.9 us -> none  [per_device(): targets = lax.psum_scatter(partial, 'cols', scatter_dimension=1, tiled=True)]
    pallas_call x1, Pallas kernels: 111 us -> 137 us  [per_device(): pl.pallas_call(kernel, out_shape=(jax.ShapeDtypeStruct((512, 1024), BF16)...]
  transfers between devices with their start and end apart: 1 -> 0, of which waited for: 1 -> 0; matrix products, arithmetic and copies ran while one was open for 0% -> 0% of each run, Pallas kernels for 0% -> 0%
where the time goes in v2:
time: 143 us; the launch traced here: 142 us
  Pallas kernels  137 us (96%)
  local copies, waits for them, and re-layouts  4.78 us (3%)
    pallas_call x1, Pallas kernels, per_device(): pl.pallas_call(kernel, out_shape=(jax.ShapeDtypeStruct((512, 1024), BF16)...  137 us
    unnamed x2, local copies, waits for them, and re-layouts  3.53 us

profile of v2, /device:TPU:1, one launch (start us, length us, event | category | flops | bytes accessed | tf_op | source)
XLA Modules:
  0.0 142.5 jit_solution(5146784415894485074)
XLA Ops:
  0.6 137.0 %shard_map.49 = (bf16[512,1024]{1,0:T(8,128)(2,1)}, f32[8,128]{1,0:T(8,128)}, f32[8,128]{1,0:T(8,128)}) custom-call(bf16[512,4096]{1,0:T(8,128)(2,1)} %noise_hbm.1, bf16[64,1024]{1,0:T(8,128)(2,1)} %bitcast.5), custom_call_target="tpu_custom_call" | custom-call | flops 17999998976 | bytes 9437184 | tf_op jit(solution)/shard_map/pallas_call | solution.py:410
  137.7 1.3 slice_bitcast_fusion
  138.9 2.3 %copy.7 = bf16[512,1024]{1,0:T(8,128)(2,1)} copy(bf16[512,1024]{1,0:T(8,128)(2,1)} %get-tuple-element.12) | data formatting | bytes 2097152
  141.2 1.3 copy.8

commit v3 on v2

--- a/solution.py
+++ b/solution.py
@@ -51,13 +51,19 @@
     whole_a[me] = data_ref[...]
     pl.semaphore_wait(barrier, 66)
 
-    def at(part, da, db):
-        return index(y + db, x + da, 0) if part == 0 else index(y + da, x + db, 1)
-
-    def near(part, da, db):
-        return index(y + db, x + da, zl) if part == 0 else index(y + da, x + db, zl)
-
-    base = (1, 25)
+    def place(p, da, db, ll):
+        return index(y + db * (1 - p) + da * p, x + da * (1 - p) + db * p, ll)
+
+    def at(p, da, db):
+        return place(p, da, db, p)
+
+    def near(p, da, db):
+        return place(p, da, db, zl)
+
+    def base(p):
+        return 1 + 24 * p
+
+    parts = (zl, 1 - zl)
     turns = (0, -1, 1, 2)
 
     class Gather:
@@ -92,60 +98,52 @@
             theirs = slot + 1 - 2 * core
             self.of_turn[n].append(self.remote(theirs, None, self.bsend.at[t], self.brecv.at[t], sibling))
 
+        def launch(self, p):
+            self.move(base(p) + 0, at(p, 0, 0), near(p, 1, 0))
+            self.move(base(p) + 1, at(p, 0, 0), near(p, -1, 0))
+            self.second(0, p)
+
         def begin(self):
             self.move(0, me, index(y, x, 1 - zl))
+            self.launch(zl)
             self.share(me, 0)
 
         def first(self):
             self.arrived(0, index(y, x, 1 - zl))
-            for part in (0, 1):
-                b = base[part]
-                self.move(b + 0, at(part, 0, 0), near(part, 1, 0))
-                self.move(b + 1, at(part, 0, 0), near(part, -1, 0))
+            self.launch(1 - zl)
             self.share(index(y, x, 1 - zl), 0)
 
-        def second(self, n):
-            for part in (0, 1):
-                b = base[part] + 4 + 5 * n
-                self.move(b + 0, at(part, turns[n], 0), near(part, 0, 1))
-                self.move(b + 1, at(part, turns[n], 0), near(part, 0, -1))
-
-        def halves(self):
-            for part in (0, 1):
-                b = base[part]
-                self.arrived(b + 0, at(part, -1, 0))
-                self.move(b + 2, at(part, -1, 0), near(part, 1, 0), 0)
-                self.arrived(b + 1, at(part, 1, 0))
-                self.move(b + 3, at(part, 1, 0), near(part, -1, 0), 1)
-
-        def share_first(self):
-            for part in (0, 1):
-                self.share(at(part, -1, 0), 1)
-                self.share(at(part, 1, 0), 2)
-
-        def opposite(self):
-            for part in (0, 1):
-                b = base[part]
-                self.arrived(b + 2, at(part, 2, 0), 0)
-                self.arrived(b + 3, at(part, 2, 0), 1)
-                self.share(at(part, 2, 0), 3)
-
-        def relay(self, n, up):
-            for part in (0, 1):
-                b = base[part] + 4 + 5 * n
-                self.arrived(b + 0, at(part, turns[n], -1))
-                if up:
-                    self.move(b + 2, at(part, turns[n], -1), near(part, 0, 1))
-                self.share(at(part, turns[n], -1), n)
-                self.arrived(b + 1, at(part, turns[n], 1))
-                if not up:
-                    self.move(b + 2, at(part, turns[n], 1), near(part, 0, -1))
-                self.share(at(part, turns[n], 1), n)
+        def second(self, n, p):
+            b = base(p) + 4 + 5 * n
+            self.move(b + 0, at(p, turns[n], 0), near(p, 0, 1))
+            self.move(b + 1, at(p, turns[n], 0), near(p, 0, -1))
+
+        def turn(self, n, p):
+            b = base(p)
+            slot = at(p, turns[n], 0)
+            if n < 3:
+                self.arrived(b + n - 1, slot)
+                self.move(b + n + 1, slot, near(p, -turns[n], 0), n - 1)
+            else:
+                self.arrived(b + 2, slot, 0)
+                self.arrived(b + 3, slot, 1)
+            self.second(n, p)
+            self.share(slot, n)
+
+        def relay(self, n, p):
+            b = base(p) + 4 + 5 * n
+            for t, db in enumerate((-1, 1)):
+                slot = at(p, turns[n], db)
+                self.arrived(b + t, slot)
+                if t == n % 2:
+                    self.move(b + 2, slot, near(p, 0, -db))
+                self.share(slot, n)
 
         def last(self, n):
-            for part in (0, 1):
-                self.arrived(base[part] + 4 + 5 * n + 2, at(part, turns[n], 2))
-                self.share(at(part, turns[n], 2), n)
+            for p in parts:
+                slot = at(p, turns[n], 2)
+                self.arrived(base(p) + 4 + 5 * n + 2, slot)
+                self.share(slot, n)
 
         def turn_done(self, n):
             for copy in self.of_turn[n]:
@@ -155,7 +153,7 @@
             for copy in self.sent:
                 copy.wait_send()
 
-    def add_gram(whole, n, keep):
+    def add_gram(whole, scores, n):
         for part in (0, 1):
             firsts = [
                 (((i * 4 + (x + turns[n] + 4) % 4) * 2 + part) * 2) if part == 0
@@ -183,25 +181,35 @@
     )
     first_block.first()
     across.start()
-    first_block.second(0)
-    first_block.halves()
-    first_block.second(1)
-    first_block.second(2)
-    first_block.share_first()
-    first_block.relay(0, True)
-    first_block.opposite()
-    first_block.second(3)
-    first_block.relay(1, False)
-    first_block.relay(2, True)
+    p, q = parts
+    first_block.turn(1, p)
+    first_block.turn(1, q)
+    first_block.turn(2, p)
+    first_block.turn(2, q)
+    first_block.relay(0, p)
+    first_block.relay(0, q)
+    first_block.turn(3, p)
+    first_block.turn(3, q)
+    first_block.relay(1, p)
+    first_block.relay(1, q)
+    first_block.relay(2, p)
+    first_block.relay(2, q)
     first_block.last(0)
-    first_block.relay(3, False)
+    first_block.relay(3, p)
+    first_block.relay(3, q)
     load.wait()
     first_block.turn_done(0)
-    add_gram(whole_a, 0, False)
-    for n in (1, 2, 3):
+    add_gram(whole_a, scores, 0)
+    across.wait()
+    other_block.begin()
+    first_block.last(1)
+    first_block.turn_done(1)
+    add_gram(whole_a, scores, 1)
+    other_block.first()
+    for n in (2, 3):
         first_block.last(n)
         first_block.turn_done(n)
-        add_gram(whole_a, n, False)
+        add_gram(whole_a, scores, n)
 
     def square_cols(i, acc):
         v = whole_a[i].astype(F32)
@@ -267,36 +275,43 @@
         everything.wait_send()
         return cbuf[e]
 
+    def other_gram(n):
+        other_block.last(n)
+        other_block.turn_done(n)
+        add_gram(whole_b, own_ref, n)
+
     def step_r1():
-        across.wait()
-        other_block.begin()
+        for p in parts:
+            other_block.turn(1, p)
 
     def step_c1():
-        other_block.first()
+        for p in parts:
+            other_block.turn(2, p)
 
     def step_r2():
-        other_block.halves()
-        other_block.second(0)
-        other_block.share_first()
+        for p in parts:
+            other_block.relay(0, p)
+            other_block.turn(3, p)
 
     def step_c2():
-        other_block.second(1)
-        other_block.opposite()
+        for p in parts:
+            other_block.relay(1, p)
 
     def step_r3():
-        other_block.second(2)
+        for p in parts:
+            other_block.relay(2, p)
 
     def step_c3():
-        other_block.relay(0, True)
-        other_block.second(3)
+        for p in parts:
+            other_block.relay(3, p)
+        other_gram(0)
 
     def step_r4():
-        other_block.relay(1, False)
-        other_block.relay(2, True)
-        other_block.last(0)
+        other_gram(1)
 
     def step_c4():
-        other_block.relay(3, False)
+        other_gram(2)
+        other_gram(3)
 
     row_steps = (step_r1, step_r2, step_r3, step_r4)
     col_steps = (step_c1, step_c2, step_c3, step_c4)
@@ -343,47 +358,43 @@
     plan_ref[:, :1024] = plan.astype(BF16)
     sums = jnp.sum(plan, axis=1, keepdims=True)
 
-    other_block.turn_done(0)
-    add_gram(whole_b, 0, False)
-    for n in (1, 2, 3):
-        other_block.last(n)
-        other_block.turn_done(n)
-        add_gram(whole_b, n, False)
+    def product(rows, half, q, c):
+        right = (whole_a, whole_b)[half][pl.ds(q * 16 + c * 4, 4)].reshape(256, 1024)
+        return lax.dot_general(
+            plan_ref[rows, pl.ds(half * 1024, 1024)], right, (((1,), (1,)), ((), ())),
+            preferred_element_type=F32,
+        )
+
+    sides = ((0, (zh + 1) % 4), (1, (zh + 3) % 4))
+    for c in range(4):
+        for d, q in sides:
+            mass[pl.ds(d * 256, 256), pl.ds(c * 256, 256)] = product(pl.ds(d * 256, 256), 0, q, c)
+
     swap.wait()
-    plan = jnp.exp2(scores[...] + row_bits + unfold(pbuf[0]))
+    plan = jnp.exp2(own_ref[...] + row_bits + unfold(pbuf[0]))
     plan_ref[:, 1024:] = plan.astype(BF16)
-    sums = compact(sums + jnp.sum(plan, axis=1, keepdims=True))
+    sums = sums + jnp.sum(plan, axis=1, keepdims=True)
+
+    hand = []
+    for c in range(4):
+        for d, q in sides:
+            rows = pl.ds(d * 256, 256)
+            part_ref[d, c] = (mass[rows, pl.ds(c * 256, 256)] + product(rows, 1, q, c)).astype(BF16)
+            copy = pltpu.make_async_remote_copy(
+                src_ref=part_ref.at[d, c], dst_ref=got_ref.at[d, c], send_sem=tsend.at[d, c],
+                recv_sem=trecv.at[d, c], device_id=(me, q), device_id_type=MESH,
+            )
+            copy.start()
+            hand.append(copy)
+    sums = compact(sums)
     pmsg[1] = sums
     tell = pltpu.make_async_remote_copy(
         src_ref=pmsg.at[1], dst_ref=pbuf.at[1], send_sem=psend.at[1], recv_sem=precv.at[1],
         device_id=(me, (zh + 1) % 4), device_id_type=MESH,
     )
     tell.start()
-
-    def product(rows, q, c):
-        total = None
-        for half, whole in ((0, whole_a), (1, whole_b)):
-            right = whole[pl.ds(q * 16 + c * 4, 4)].reshape(256, 1024)
-            value = lax.dot_general(
-                plan_ref[rows, pl.ds(half * 1024, 1024)], right, (((1,), (1,)), ((), ())),
-                preferred_element_type=F32,
-            )
-            total = value if total is None else total + value
-        return total
-
-    hand = []
     for c in range(4):
-        for d, step in ((0, 1), (1, 3)):
-            q = (zh + step) % 4
-            part_ref[d, c] = product(pl.ds(d * 256, 256), q, c).astype(BF16)
-            copy = pltpu.make_async_remote_copy(
-                src_ref=part_ref.at[d, c], dst_ref=got_ref.at[d, c], send_sem=tsend.at[d, c],
-                recv_sem=trecv.at[d, c], device_id=(me, q), device_id_type=MESH,
-            )
-            copy.start()
-            hand.append(copy)
-    for c in range(4):
-        own_ref[:, pl.ds(c * 256, 256)] = product(pl.ds(0, 512), zh, c)
+        own_ref[:, pl.ds(c * 256, 256)] = product(pl.ds(0, 512), 0, zh, c) + product(pl.ds(0, 512), 1, zh, c)
 
     v = noise_ref[...].astype(F32)
     noise_sq = compact(jnp.sum(v * v, axis=1, keepdims=True))
@@ -402,6 +413,14 @@
         copy.wait_send()
     first_block.done()
     other_block.done()
+
+
+def deliver(targets_ref, row_ref, col_ref, targets_out, row_out, col_out):
+    targets_out[...] = targets_ref[...]
+    for i in range(4):
+        row_out[pl.ds(i * 128, 128)] = row_ref[i]
+    for i in range(8):
+        col_out[pl.ds(i * 128, 128)] = col_ref[i]
 
 
 def per_device(noise, data):
@@ -451,7 +470,16 @@
         ),
         cost_estimate=pl.CostEstimate(flops=18 * 10**9, bytes_accessed=9 * 2**20, transcendentals=3 * 10**6),
     )(noise, data.T)
-    return targets, row_pot[:4].reshape(512), col_pot.reshape(1024)
+    return pl.pallas_call(
+        deliver,
+        out_shape=(
+            jax.ShapeDtypeStruct((512, 1024), BF16),
+            jax.ShapeDtypeStruct((512,), F32),
+            jax.ShapeDtypeStruct((1024,), F32),
+        ),
+        in_specs=[vmem, vmem, vmem],
+        out_specs=(vmem, vmem, vmem),
+    )(targets, row_pot, col_pot)
 
 
 def solution(mesh):

time: 143 us -> 133 us (0.930)
  Pallas kernels: 137 us -> 132 us
  local copies, waits for them, and re-layouts: 4.78 us -> 0 us
    pallas_call x1, Pallas kernels: 137 us -> 130 us  [per_device(): pl.pallas_call(kernel, out_shape=(jax.ShapeDtypeStruct((512, 1024), BF16)...]
    unnamed x2 -> x0, local copies, waits for them, and re-layouts: 3.53 us -> none
    pallas_call x0 -> x1, Pallas kernels: none -> 2.28 us  [per_device(): pl.pallas_call(deliver, out_shape=(jax.ShapeDtypeStruct((512, 1024), BF16...]
where the time goes in v3:
time: 133 us; the launch traced here: 132 us
  Pallas kernels  132 us (99%)
    pallas_call x1, Pallas kernels, per_device(): pl.pallas_call(kernel, out_shape=(jax.ShapeDtypeStruct((512, 1024), BF16)...  130 us

profile of v3, /device:TPU:1, one launch (start us, length us, event | category | flops | bytes accessed | tf_op | source)
XLA Modules:
  0.0 132.5 jit_solution(12088703142332224421)
XLA Ops:
  0.6 129.6 %shard_map.49 = (bf16[512,1024]{1,0:T(8,128)(2,1)}, f32[8,128]{1,0:T(8,128)}, f32[8,128]{1,0:T(8,128)}) custom-call(bf16[512,4096]{1,0:T(8,128)(2,1)} %noise_hbm.1, bf16[64,1024]{1,0:T(8,128)(2,1)} %bitcast.1), custom_call_target="tpu_custom_call" | custom-call | flops 17999998976 | bytes 9437184 | tf_op jit(solution)/shard_map/pallas_call | solution.py:429
  130.2 2.3 %shard_map.50 = (bf16[512,1024]{1,0:T(8,128)(2,1)}, f32[512]{0:T(512)}, f32[1024]{0:T(1024)}) custom-call(bf16[512,1024]{1,0:T(8,128)(2,1)} %get-tuple-element.6.targets_ref, f32[8,128]{1,0:T(8,128)} %get-tuple-element.7.row_ref, f32[8,128]{1,0:T(8,128)} %get-tuple-element.8.col_ref), custom_call_target="tpu_custom_call" | custom-call | tf_op jit(solution)/shard_map/pallas_call | solution.py:473

commit v4 on v3

--- a/solution.py
+++ b/solution.py
@@ -21,7 +21,7 @@
     noise_hbm, data_ref, out_ref, row_ref, col_ref,
     noise_ref, whole_a, whole_b, scores, mass, plan_ref, part_ref, got_ref, own_ref,
     rmsg, rbuf, cmsg, cbuf, pmsg, pbuf,
-    nsem, zsend, zrecv, asems, bsems, rsend, rrecv, csend, crecv, psend, precv, tsend, trecv,
+    news, nsem, zsend, zrecv, asems, bsems, rsend, rrecv, csend, crecv, psend, precv, tsend, trecv,
 ):
     rows_total = 32768
     cols_total = 4096
@@ -39,17 +39,16 @@
     load = pltpu.make_async_copy(noise_hbm, noise_ref, nsem)
     load.start()
 
+    above = (index(y, x, 1 - zl), lax.rem(zh + zl, 4))
+    below = (index(y, x, 1 - zl), lax.rem(zh + 3 + zl, 4))
     barrier = pltpu.get_barrier_semaphore()
-
-    def greet(o, carry):
-        pl.semaphore_signal(barrier, inc=1, device_id=((me + o) % 64, zh), device_id_type=MESH)
-        return carry
-
-    lax.fori_loop(1, 64, greet, 0)
-    for o in range(1, 4):
-        pl.semaphore_signal(barrier, inc=1, device_id=(me, (zh + o) % 4), device_id_type=MESH)
+    for step in ((1, 0), (-1, 0), (0, 1), (0, -1)):
+        beside = (index(y + step[0], x + step[1], zl), zh)
+        pl.semaphore_signal(barrier, inc=1, device_id=beside, device_id_type=MESH)
+    for beside in (above, below, (sibling, zh)):
+        pl.semaphore_signal(barrier, inc=1, device_id=beside, device_id_type=MESH)
     whole_a[me] = data_ref[...]
-    pl.semaphore_wait(barrier, 66)
+    pl.semaphore_wait(barrier, 7)
 
     def place(p, da, db, ll):
         return index(y + db * (1 - p) + da * p, x + da * (1 - p) + db * p, ll)
@@ -179,13 +178,19 @@
         src_ref=whole_a.at[me], dst_ref=whole_b.at[me], send_sem=zsend, recv_sem=zrecv,
         device_id=(me, (zh + 2) % 4), device_id_type=MESH,
     )
+    pl.semaphore_signal(news.at[0], inc=1, device_id=below, device_id_type=MESH)
+    pl.semaphore_signal(news.at[1], inc=1, device_id=above, device_id_type=MESH)
     first_block.first()
-    across.start()
+    pl.semaphore_wait(news.at[0], 1)
+    pl.semaphore_wait(news.at[1], 1)
+    pl.semaphore_signal(news.at[2], inc=1, device_id=(me, (zh + 3) % 4), device_id_type=MESH)
     p, q = parts
     first_block.turn(1, p)
     first_block.turn(1, q)
     first_block.turn(2, p)
     first_block.turn(2, q)
+    pl.semaphore_wait(news.at[2], 1)
+    across.start()
     first_block.relay(0, p)
     first_block.relay(0, q)
     first_block.turn(3, p)
@@ -451,6 +456,7 @@
             pltpu.VMEM((ITERS, 63, 8, 128), F32),
             pltpu.VMEM((2, 8, 128), F32),
             pltpu.VMEM((2, 8, 128), F32),
+            pltpu.SemaphoreType.REGULAR((3,)),
             dma,
             dma,
             dma,

time: 133 us -> 129 us (0.970)
  Pallas kernels: 132 us -> 128 us
    pallas_call x1, Pallas kernels: 130 us -> 126 us  [per_device(): pl.pallas_call(kernel, out_shape=(jax.ShapeDtypeStruct((512, 1024), BF16)...]
where the time goes in v4:
time: 129 us
  Pallas kernels  128 us (99%)
    pallas_call x1, Pallas kernels, per_device(): pl.pallas_call(kernel, out_shape=(jax.ShapeDtypeStruct((512, 1024), BF16)...  126 us

profile of v4, /device:TPU:1, one launch (start us, length us, event | category | flops | bytes accessed | tf_op | source)
XLA Modules:
  0.0 129.0 jit_solution(12434943047599242388)
XLA Ops:
  0.6 126.1 %shard_map.49 = (bf16[512,1024]{1,0:T(8,128)(2,1)}, f32[8,128]{1,0:T(8,128)}, f32[8,128]{1,0:T(8,128)}) custom-call(bf16[512,4096]{1,0:T(8,128)(2,1)} %noise_hbm.1, bf16[64,1024]{1,0:T(8,128)(2,1)} %bitcast.1), custom_call_target="tpu_custom_call" | custom-call | flops 17999998976 | bytes 9437184 | tf_op jit(solution)/shard_map/pallas_call | solution.py:434
  126.7 2.3 %shard_map.50 = (bf16[512,1024]{1,0:T(8,128)(2,1)}, f32[512]{0:T(512)}, f32[1024]{0:T(1024)}) custom-call(bf16[512,1024]{1,0:T(8,128)(2,1)} %get-tuple-element.6.targets_ref, f32[8,128]{1,0:T(8,128)} %get-tuple-element.7.row_ref, f32[8,128]{1,0:T(8,128)} %get-tuple-element.8.col_ref), custom_call_target="tpu_custom_call" | custom-call | tf_op jit(solution)/shard_map/pallas_call | solution.py:479

commit v5 on v4

--- a/solution.py
+++ b/solution.py
@@ -205,8 +205,7 @@
     load.wait()
     first_block.turn_done(0)
     add_gram(whole_a, scores, 0)
-    across.wait()
-    other_block.begin()
+    across.wait(); other_block.begin()
     first_block.last(1)
     first_block.turn_done(1)
     add_gram(whole_a, scores, 1)
@@ -296,9 +295,10 @@
     def step_r2():
         for p in parts:
             other_block.relay(0, p)
+
+    def step_c2():
+        for p in parts:
             other_block.turn(3, p)
-
-    def step_c2():
         for p in parts:
             other_block.relay(1, p)
 

time: 129 us -> 127 us (0.984)
  Pallas kernels: 128 us -> 126 us
    pallas_call x1, Pallas kernels: 126 us -> 124 us  [per_device(): pl.pallas_call(kernel, out_shape=(jax.ShapeDtypeStruct((512, 1024), BF16)...]
where the time goes in v5:
time: 127 us
  Pallas kernels  126 us (99%)
    pallas_call x1, Pallas kernels, per_device(): pl.pallas_call(kernel, out_shape=(jax.ShapeDtypeStruct((512, 1024), BF16)...  124 us

profile of v5, /device:TPU:1, one launch (start us, length us, event | category | flops | bytes accessed | tf_op | source)
XLA Modules:
  0.0 127.1 jit_solution(7159185620265567499)
XLA Ops:
  0.6 124.2 %shard_map.49 = (bf16[512,1024]{1,0:T(8,128)(2,1)}, f32[8,128]{1,0:T(8,128)}, f32[8,128]{1,0:T(8,128)}) custom-call(bf16[512,4096]{1,0:T(8,128)(2,1)} %noise_hbm.1, bf16[64,1024]{1,0:T(8,128)(2,1)} %bitcast.1), custom_call_target="tpu_custom_call" | custom-call | flops 17999998976 | bytes 9437184 | tf_op jit(solution)/shard_map/pallas_call | solution.py:434
  124.8 2.3 %shard_map.50 = (bf16[512,1024]{1,0:T(8,128)(2,1)}, f32[512]{0:T(512)}, f32[1024]{0:T(1024)}) custom-call(bf16[512,1024]{1,0:T(8,128)(2,1)} %get-tuple-element.6.targets_ref, f32[8,128]{1,0:T(8,128)} %get-tuple-element.7.row_ref, f32[8,128]{1,0:T(8,128)} %get-tuple-element.8.col_ref), custom_call_target="tpu_custom_call" | custom-call | tf_op jit(solution)/shard_map/pallas_call | solution.py:479
